TPU v7x, 512 devices: a whole 4x4x16 slice. The times are simulated.
512 devices in a mesh: row: 16 (over z_lo, x), col: 32 (over z_hi, y, core).
Axes of the slice: x: 4, y: 4, z: 16 (z_hi: 4, z_lo: 4; z = z_hi * 4 + z_lo), core: 2. Of those that a mesh axis runs over, the one named last changes fastest.
Arguments:
- left_points: float32 [32768, 128], P(('row', 'col')), may hold values from -3.3 to 3.3
- right_points: float32 [32768, 128], P(('row', 'col')), may hold values from -3.3 to 3.3
- left_cotangent: bfloat16 [32768, 128], P(('row', 'col')), may hold values from -6 to 6
- right_coefficient: bfloat16 [32768, 128], P(('row', 'col')), may hold values from -6 to 6
Outputs:
- left_final: float32 [32768, 128], P(('row', 'col'))
- right_final: float32 [32768, 128], P(('row', 'col'))
- left_grad: float32 [32768, 128], P(('row', 'col'))
- right_grad: float32 [32768, 128], P(('row', 'col'))
All inputs are finite; a program needn't handle non-finite values.
Results may differ from a plain program's by a relative error of at most 0.019.
Values may be sent and summed in bfloat16 or wider, within the bound.
A program may use at most 64 MiB of HBM per device.

v0:
```python
import jax
import jax.numpy as jnp
from jax import lax
from jax.sharding import PartitionSpec as P

STEPS = 2


inverse_width = 0.03125
grad_scale = 0.0625
descent_rate = 0.3


def copy_for_each(shard, axis):
    length = lax.axis_size(axis)
    return lax.all_to_all(
        jnp.broadcast_to(shard[None], (length, *shard.shape)), axis, 0, 0, tiled=True
    )


def in_order(blocks, dim):
    dims = list(blocks.shape[1:])
    dims[dim] *= blocks.shape[0]
    return jnp.moveaxis(blocks, 0, dim).reshape(dims)


def gather_directly(shard, axis, dim):
    blocks = copy_for_each(shard, axis)
    return in_order(blocks, dim)


def cut_along(shard, dim, length):
    before, after = (shard.shape[:dim], shard.shape[dim + 1 :])
    return jnp.moveaxis(shard.reshape(*before, length, -1, *after), dim, 0)


def sent_and_summed(shard, axis, dim):
    blocks = cut_along(shard, dim, lax.axis_size(axis))
    arrived = lax.all_to_all(blocks, axis, split_axis=0, concat_axis=0, tiled=True)
    return arrived.sum(axis=0)


def tile_terms(left_bf, left_panel, right_bf, right_panel):
    left_rows = left_bf.shape[0]
    block_rows = min(512, left_rows)
    block_count = left_rows // block_rows
    feature_width = left_bf.shape[1]
    right_wide = right_bf.astype(jnp.float32)
    right_norm = jnp.sum(right_wide * right_wide, axis=1)
    contract_last = (((1,), (1,)), ((), ()))

    def visit_block(carried, pieces):
        accumulated, column_sum = carried
        piece_feat, piece_panel = pieces
        piece_wide = piece_feat.astype(jnp.float32)
        left_norm = jnp.sum(piece_wide * piece_wide, axis=1)
        crossed = lax.dot_general(
            piece_feat, right_bf, contract_last, preferred_element_type=jnp.float32
        )
        distance = left_norm[:, None] + right_norm[None, :] - 2.0 * crossed
        kernel = jnp.exp(-inverse_width * distance).astype(jnp.bfloat16)
        weight = lax.dot_general(
            piece_panel, right_panel, contract_last, preferred_element_type=jnp.float32
        )
        product = (weight * kernel.astype(jnp.float32)).astype(jnp.bfloat16)
        product_wide = product.astype(jnp.float32)
        left_term = (
            jnp.dot(product, right_bf, preferred_element_type=jnp.float32)
            - jnp.sum(product_wide, axis=1)[:, None] * piece_wide
        )
        accumulated = accumulated + lax.dot_general(
            product, piece_feat, (((0,), (0,)), ((), ())), preferred_element_type=jnp.float32
        )
        column_sum = column_sum + jnp.sum(product_wide, axis=0)
        return ((accumulated, column_sum), left_term)

    initial = (
        jnp.zeros((right_bf.shape[0], feature_width), jnp.float32),
        jnp.zeros((right_bf.shape[0],), jnp.float32),
    )
    pieces = (
        left_bf.reshape(block_count, block_rows, feature_width),
        left_panel.reshape(block_count, block_rows, left_panel.shape[1]),
    )
    (accumulated, column_sum), left_terms = lax.scan(visit_block, initial, pieces)
    return (
        left_terms.reshape(left_rows, feature_width),
        accumulated - column_sum[:, None] * right_wide,
    )


def body(left_points, right_points, left_cotangent, right_coefficient):
    left_panel = lax.all_gather(left_cotangent, "col", axis=0, tiled=True)
    right_panel = gather_directly(right_coefficient, "row", 0)
    left_own = left_points
    right_own = right_points
    left_grad = jnp.zeros_like(left_points)
    right_grad = jnp.zeros_like(right_points)
    for step_index in range(STEPS):
        left_bf = gather_directly(left_own.astype(jnp.bfloat16), "col", 0)
        right_bf = gather_directly(right_own.astype(jnp.bfloat16), "row", 0)
        left_term, right_term = tile_terms(left_bf, left_panel, right_bf, right_panel)
        if step_index + 1 < STEPS:
            left_step = sent_and_summed(left_term, "col", 0) * grad_scale
            right_step = sent_and_summed(right_term, "row", 0) * grad_scale
            left_own = left_own - descent_rate * left_step
            right_own = right_own - descent_rate * right_step
        else:
            left_grad = (
                lax.psum_scatter(left_term, "col", scatter_dimension=0, tiled=True) * grad_scale
            )
            right_grad = sent_and_summed(right_term, "row", 0) * grad_scale
            left_own = left_own - descent_rate * left_grad
            right_own = right_own - descent_rate * right_grad
    return (left_own, right_own, left_grad, right_grad)


def solution(mesh):
    in_specs = (
        P(("row", "col"), None),
        P(("row", "col"), None),
        P(("row", "col"), None),
        P(("row", "col"), None),
    )
    out_specs = (
        P(("row", "col"), None),
        P(("row", "col"), None),
        P(("row", "col"), None),
        P(("row", "col"), None),
    )
    return jax.shard_map(body, mesh=mesh, in_specs=in_specs, out_specs=out_specs, check_vma=False)
```

profile of v0, /device:TPU:1, one launch (start us, length us, event | category | flops | bytes accessed | tf_op | source)
XLA Modules:
  0.0 425.4 jit_solution(1048036105531384965)
XLA Ops:
  7.2 0.8 convert_element_type.55
  8.0 18.3 %all_to_all.40 = bf16[16,64,128]{2,1,0:T(8,128)(2,1)S(1)} all-to-all(bf16[16,64,128]{2,1,0:T(8,128)(2,1)S(1)} %broadcast_in_dim.22), channel_id=1, replica_groups=mesh['row'=16,'col'=32] {'row'}, dimensions={0} | all-to-all | bytes 524288 | tf_op jit(solution)/shard_map/all_to_all | solution.py:16
  26.3 1.5 broadcast_in_dim.20
  27.8 4.3 %all-to-all-start = ((bf16[16,64,128]{2,1,0:T(8,128)(2,1)}), bf16[16,64,128]{2,1,0:T(8,128)(2,1)S(1)}, u32[]{:S(2)}, u32[]{:S(2)}) async-start(bf16[16,64,128]{2,1,0:T(8,128)(2,1)} %broadcast_in_dim.20), calls=%async_computation | async-start | bytes 524288 | tf_op jit(solution)/shard_map/all_to_all | solution.py:16
  32.1 8.8 %all-to-all-done = bf16[16,64,128]{2,1,0:T(8,128)(2,1)S(1)} async-done(((bf16[16,64,128]{2,1,0:T(8,128)(2,1)}), bf16[16,64,128]{2,1,0:T(8,128)(2,1)S(1)}, u32[]{:S(2)}, u32[]{:S(2)}) %all-to-all-start) | async-done | bytes 262176 | tf_op jit(solution)/shard_map/all_to_all | solution.py:16
  40.9 0.9 broadcast_in_dim.21
  41.8 18.1 %all-to-all-start.1 = ((bf16[32,64,128]{2,1,0:T(8,128)(2,1)}), bf16[32,64,128]{2,1,0:T(8,128)(2,1)S(1)}, u32[]{:S(2)}, u32[]{:S(2)}) async-start(bf16[32,64,128]{2,1,0:T(8,128)(2,1)} %broadcast_in_dim.21), calls=%async_computation.1 | async-start | bytes 1048576 | tf_op jit(solution)/shard_map/all_to_all | solution.py:16
  59.9 72.2 %all_gather.3 = bf16[2048,128]{1,0:T(8,128)(2,1)S(1)} all-gather(bf16[64,128]{1,0:T(8,128)(2,1)S(1)} %copy-done.2), channel_id=1, replica_groups=mesh['row'=16,'col'=32] {'col'}, dimensions={0}, use_global_device_ids=true | all-gather | bytes 540672 | tf_op jit(solution)/shard_map/all_gather | solution.py:93
  132.4 1.1 broadcast.44.clone
  133.4 12.6 %while.30 = (s32[]{:T(128)}, f32[1024,128]{1,0:T(8,128)S(1)}, f32[1024]{0:T(1024)S(1)}, f32[4,512,128]{2,1,0:T(8,128)}, bf16[4,512,128]{2,1,0:T(8,128)(2,1)S(1)}...) while((s32[]{:T(128)}, f32[1024,128]{1,0:T(8,128)S(1)}, ...), condition=%wide.region_5.6_spmd.clone, body=%wide.region_1.5_spmd.clone.sunk | while | flops 543293440 | bytes 8024712 | solution.py:85
  134.8 1.1 fusion.62
  137.9 1.2 fusion.62
  141.1 1.2 fusion.62
  144.3 1.2 fusion.62
  146.3 17.2 %all_to_all.41 = f32[16,64,128]{2,1,0:T(8,128)S(1)} all-to-all(f32[16,64,128]{2,1,0:T(8,128)S(1)} %bitcast.106), channel_id=1, replica_groups=mesh['row'=16,'col'=32] {'row'}, dimensions={0} | all-to-all | bytes 1048576 | tf_op jit(solution)/shard_map/all_to_all | solution.py:39
  163.5 12.5 %all-to-all-start.3 = ((f32[32,64,128]{2,1,0:T(8,128)}), f32[32,64,128]{2,1,0:T(8,128)S(1)}, u32[]{:S(2)}, u32[]{:S(2)}) async-start(f32[32,64,128]{2,1,0:T(8,128)} %bitcast.4), calls=%async_computation.3 | async-start | bytes 2097152 | tf_op jit(solution)/shard_map/all_to_all | solution.py:39
  176.1 38.6 %all-to-all-done.3 = f32[32,64,128]{2,1,0:T(8,128)S(1)} async-done(((f32[32,64,128]{2,1,0:T(8,128)}), f32[32,64,128]{2,1,0:T(8,128)S(1)}, u32[]{:S(2)}, u32[]{:S(2)}) %all-to-all-start.3) | async-done | bytes 1048608 | tf_op jit(solution)/shard_map/all_to_all | solution.py:39
  215.5 19.9 %all-to-all-start.6 = ((bf16[16,64,128]{2,1,0:T(8,128)(2,1)}), bf16[16,64,128]{2,1,0:T(8,128)(2,1)S(1)}, u32[]{:S(2)}, u32[]{:S(2)}) async-start(bf16[16,64,128]{2,1,0:T(8,128)(2,1)} %broadcast_in_dim.24), calls=%async_computation.6 | async-start | bytes 524288 | tf_op jit(solution)/shard_map/all_to_all | solution.py:16
  235.5 9.6 %all-to-all-done.6 = bf16[16,64,128]{2,1,0:T(8,128)(2,1)S(1)} async-done(((bf16[16,64,128]{2,1,0:T(8,128)(2,1)}), bf16[16,64,128]{2,1,0:T(8,128)(2,1)S(1)}, u32[]{:S(2)}, u32[]{:S(2)}) %all-to-all-start.6) | async-done | bytes 262176 | tf_op jit(solution)/shard_map/all_to_all | solution.py:16
  245.1 0.9 broadcast_in_dim.23
  246.0 7.4 %all-to-all-start.4 = ((bf16[32,64,128]{2,1,0:T(8,128)(2,1)}), bf16[32,64,128]{2,1,0:T(8,128)(2,1)S(1)}, u32[]{:S(2)}, u32[]{:S(2)}) async-start(bf16[32,64,128]{2,1,0:T(8,128)(2,1)} %broadcast_in_dim.23), calls=%async_computation.4 | async-start | bytes 1048576 | tf_op jit(solution)/shard_map/all_to_all | solution.py:16
  253.7 29.8 %all-to-all-done.4 = bf16[32,64,128]{2,1,0:T(8,128)(2,1)S(1)} async-done(((bf16[32,64,128]{2,1,0:T(8,128)(2,1)}), bf16[32,64,128]{2,1,0:T(8,128)(2,1)S(1)}, u32[]{:S(2)}, u32[]{:S(2)}) %all-to-all-start.4) | async-done | bytes 524320 | tf_op jit(solution)/shard_map/all_to_all | solution.py:16
  283.5 1.1 broadcast.44
  284.6 12.7 %while.31 = (s32[]{:T(128)}, f32[1024,128]{1,0:T(8,128)S(1)}, f32[1024]{0:T(1024)S(1)}, f32[4,512,128]{2,1,0:T(8,128)}, bf16[4,512,128]{2,1,0:T(8,128)(2,1)S(1)}...) while((s32[]{:T(128)}, f32[1024,128]{1,0:T(8,128)S(1)}, ...), condition=%wide.region_13.14_spmd.clone, body=%wide.region_9.13_spmd.clone.sunk | while | flops 543293440 | bytes 8024712 | solution.py:85
  285.9 1.2 fusion.71
  289.1 1.2 fusion.71
  292.3 1.2 fusion.71
  295.5 1.2 fusion.71
  297.3 1.0 multiply_subtract_fusion
  298.3 6.5 %all-to-all-start.7 = ((f32[16,64,128]{2,1,0:T(8,128)}), f32[16,64,128]{2,1,0:T(8,128)S(1)}, u32[]{:S(2)}, u32[]{:S(2)}) async-start(f32[16,64,128]{2,1,0:T(8,128)} %bitcast.9), calls=%async_computation.8 | async-start | bytes 1048576 | tf_op jit(solution)/shard_map/all_to_all | solution.py:39
  305.6 110.9 %reduce-scatter.2.cloned.1.call-done = f32[64,128]{1,0:T(8,128)} async-done(((f32[2048,128]{1,0:T(8,128)}), f32[64,128]{1,0:T(8,128)}) %reduce-scatter.2.cloned.1.call-update) | async-done | bytes 32784 | tf_op jit(solution)/shard_map/reduce_scatter | solution.py:110
  416.5 1.4 broadcast_multiply_fusion.1
  (68 shorter events, 18.9 us)
Async XLA Ops:
  7.2 24.9 %copy-start = (f32[64,128]{1,0:T(8,128)S(1)}, f32[64,128]{1,0:T(8,128)}, u32[]{:S(2)}) copy-start(f32[64,128]{1,0:T(8,128)} %param.8) | copy-start | bytes 98308
  27.8 32.1 %copy-start.2 = (bf16[64,128]{1,0:T(8,128)(2,1)S(1)}, bf16[64,128]{1,0:T(8,128)(2,1)}, u32[]{:S(2)}) copy-start(bf16[64,128]{1,0:T(8,128)(2,1)} %param.10) | copy-start | bytes 49156
  27.8 13.2 %all-to-all-start = ((bf16[16,64,128]{2,1,0:T(8,128)(2,1)}), bf16[16,64,128]{2,1,0:T(8,128)(2,1)S(1)}, u32[]{:S(2)}, u32[]{:S(2)}) async-start(bf16[16,64,128]{2,1,0:T(8,128)(2,1)} %broadcast_in_dim.20), calls=%async_computation | async-start | bytes 524288 | tf_op jit(solution)/shard_map/all_to_all | solution.py:16
  41.8 90.5 %all-to-all-start.1 = ((bf16[32,64,128]{2,1,0:T(8,128)(2,1)}), bf16[32,64,128]{2,1,0:T(8,128)(2,1)S(1)}, u32[]{:S(2)}, u32[]{:S(2)}) async-start(bf16[32,64,128]{2,1,0:T(8,128)(2,1)} %broadcast_in_dim.21), calls=%async_computation.1 | async-start | bytes 1048576 | tf_op jit(solution)/shard_map/all_to_all | solution.py:16
  163.5 12.6 %copy-start.1 = (f32[64,128]{1,0:T(8,128)S(1)}, f32[64,128]{1,0:T(8,128)}, u32[]{:S(2)}) copy-start(f32[64,128]{1,0:T(8,128)} %param.9) | copy-start | bytes 98308
  163.5 51.2 %all-to-all-start.3 = ((f32[32,64,128]{2,1,0:T(8,128)}), f32[32,64,128]{2,1,0:T(8,128)S(1)}, u32[]{:S(2)}, u32[]{:S(2)}) async-start(f32[32,64,128]{2,1,0:T(8,128)} %bitcast.4), calls=%async_computation.3 | async-start | bytes 2097152 | tf_op jit(solution)/shard_map/all_to_all | solution.py:39
  215.5 29.6 %all-to-all-start.6 = ((bf16[16,64,128]{2,1,0:T(8,128)(2,1)}), bf16[16,64,128]{2,1,0:T(8,128)(2,1)S(1)}, u32[]{:S(2)}, u32[]{:S(2)}) async-start(bf16[16,64,128]{2,1,0:T(8,128)(2,1)} %broadcast_in_dim.24), calls=%async_computation.6 | async-start | bytes 524288 | tf_op jit(solution)/shard_map/all_to_all | solution.py:16
  246.0 37.5 %all-to-all-start.4 = ((bf16[32,64,128]{2,1,0:T(8,128)(2,1)}), bf16[32,64,128]{2,1,0:T(8,128)(2,1)S(1)}, u32[]{:S(2)}, u32[]{:S(2)}) async-start(bf16[32,64,128]{2,1,0:T(8,128)(2,1)} %broadcast_in_dim.23), calls=%async_computation.4 | async-start | bytes 1048576 | tf_op jit(solution)/shard_map/all_to_all | solution.py:16
  298.3 119.6 %all-to-all-start.7 = ((f32[16,64,128]{2,1,0:T(8,128)}), f32[16,64,128]{2,1,0:T(8,128)S(1)}, u32[]{:S(2)}, u32[]{:S(2)}) async-start(f32[16,64,128]{2,1,0:T(8,128)} %bitcast.9), calls=%async_computation.8 | async-start | bytes 1048576 | tf_op jit(solution)/shard_map/all_to_all | solution.py:39
  304.9 111.6 %reduce-scatter.2.cloned.1.call-start = ((), (), s32[]{:S(2)}) async-start(), calls=%async_computation.9 | async-start | bytes 1081344 | tf_op jit(solution)/shard_map/reduce_scatter | solution.py:110
Sparse Core Ops, SparseCore 0:
  310.1 106.3 reduce-scatter.1
where the time goes:
time: 428 us; the launch traced here: 425 us
  waiting for transfers between devices  198 us (46%)
  blocking collectives  108 us (25%)
  starting transfers between devices  68.8 us (16%)
  matrix products  23.8 us (6%)
  between operations  14.2 us (3%)
  local copies, waits for them, and re-layouts  6.34 us (1%)
  other arithmetic  5.85 us (1%)
    reduce_scatter x1, waiting for transfers between devices, body(): lax.psum_scatter(left_term, 'col', scatter_dimension=0, tiled=True)  111 us
    all_gather x1, blocking collectives, body(): left_panel = lax.all_gather(left_cotangent, 'col', axis=0, tiled=True)  72.2 us
    all_to_all x4, starting transfers between devices, copy_for_each(): lax.all_to_all(jnp.broadcast_to(shard[None], (length, *shard.shape)), axi...  49.7 us
    all_to_all x4, waiting for transfers between devices, copy_for_each(): lax.all_to_all(jnp.broadcast_to(shard[None], (length, *shard.shape)), axi...  48.2 us
    all_to_all x2, waiting for transfers between devices, sent_and_summed(): lax.all_to_all(blocks, axis, split_axis=0, concat_axis=0, tiled=True)  38.6 us
    all_to_all x2, starting transfers between devices, sent_and_summed(): lax.all_to_all(blocks, axis, split_axis=0, concat_axis=0, tiled=True)  19.1 us
    all_to_all x1, blocking collectives, copy_for_each(): lax.all_to_all(jnp.broadcast_to(shard[None], (length, *shard.shape)), axi...  18.3 us
    all_to_all x1, blocking collectives, sent_and_summed(): lax.all_to_all(blocks, axis, split_axis=0, concat_axis=0, tiled=True)  17.2 us
  transfers between devices with their start and end apart: 7, of which 5 were waited for; matrix products, arithmetic and copies ran while one was open for 0% of the time, Pallas kernels for 0%

commit v1 on v0

v1 whole, which is shorter than its diff:
```python
import jax
import jax.numpy as jnp
from jax import lax
from jax.experimental import pallas as pl
from jax.experimental.pallas import tpu as pltpu
from jax.sharding import PartitionSpec as P

STEPS = 2
LOG2E = 1.4426950408889634
PAIR_SCALE = 0.0625 * LOG2E
GRAD_SCALE = 0.0625
RATE = 0.3
MESH = pl.DeviceIdType.MESH
LAST = (((1,), (1,)), ((), ()))

Z_NEAR = (-4, 3, -3, 2, -2, 1, -1)
R_STEP = ((-1, -4), (-1, 4), (1, -4), (1, 4))
X_STEP = (0, 2, 1, 3)


def pair_kernel(lp, rp, lc, rc, lf, rf, lg, rg, lv, rv, gl, gr, own_r, la, lat, ra, rt, prod, kept, lacc, racc,
                ls, lrecv, lhs, lh, rs, rrecv, rhs, rh,
                in_sem, zs, zr, ys, yr, qs, qr, xs, xr, as_, ar, bs, br, cs, cr, ds, dr):
    row, col = lax.axis_index("row"), lax.axis_index("col")
    x, k = row % 4, col % 2
    y = (col // 2) % 4
    z = (col // 8) * 4 + row // 4

    def at(x, y, z, k):
        y, z = (y + 4) % 4, (z + 16) % 16
        return ((z % 4) * 4 + x % 4, (z // 4) * 8 + y * 2 + k)

    side = 2 * k - 1
    relays = (at(x, y, z, 1 - k), at(x, y + side, z, k), at(x, y + side, z, 1 - k))
    sources = (at(x, y, z, 1 - k), at(x, y + 1, z, 0), at(x, y - 1, z, 1))

    barrier = pltpu.get_barrier_semaphore()
    partners = [at(x, y, z + d, k) for d in (-4, -3, -2, -1, 1, 2, 3, 4)]
    partners += [at(x, y, z, 1 - k), at(x, y + side, z, k), at(x, y + side, z, 1 - k), at(x, y - side, z, k)]
    partners += [at(x, y + dy, z + dz, k) for dy, dz in R_STEP]
    partners += [at(x + dx, y, z, k) for dx in (1, 2, 3)]
    for p in partners:
        pl.semaphore_signal(barrier, inc=1, device_id=p, device_id_type=MESH)

    loads = [
        pltpu.make_async_copy(lp, lv, in_sem.at[0]),
        pltpu.make_async_copy(rp, rv, in_sem.at[1]),
        pltpu.make_async_copy(lc, gl.at[2, 0, 4], in_sem.at[2]),
        pltpu.make_async_copy(rc, own_r.at[2], in_sem.at[3]),
    ]
    for c in loads:
        c.start()
    lat[128:144, :] = jnp.ones((16, 2048), jnp.bfloat16)
    for c in loads:
        c.wait()
    gl[0, 0, 4] = lv[...].astype(jnp.bfloat16)
    own_r[0] = rv[...].astype(jnp.bfloat16)
    pl.semaphore_wait(barrier, len(partners))

    def send(src, dst, s, r, device):
        return pltpu.make_async_remote_copy(
            src_ref=src, dst_ref=dst, send_sem=s, recv_sem=r, device_id=device, device_id_type=MESH
        )

    def r_first(ph, s):
        dy, dz = R_STEP[s]
        return send(own_r.at[ph], gr.at[ph, 0, s], qs.at[ph, s], qr.at[ph, s], at(x, y - dy, z - dz, k))

    def l_first(ph, d):
        return send(gl.at[ph, 0, 4], gl.at[ph, 0, d + 4], zs.at[ph, d + 4], zr.at[ph, d + 4], at(x, y, z - d, k))

    def l_second(ph, t):
        c = 1 if t == 0 else 2 + k
        return send(gl.at[ph, 0], gl.at[ph, c], ys.at[ph, t], yr.at[ph, c - 1], relays[t])

    def l_arrived(ph, c):
        return send(gl.at[ph, 0], gl.at[ph, c], ys.at[ph, 0], yr.at[ph, c - 1], relays[0])

    def r_second(ph, i):
        return send(gr.at[ph, 0], gr.at[ph, i], xs.at[ph, i], xr.at[ph, i], at(x + X_STEP[i], y, z, k))

    def gather_start(ph):
        for s in range(4):
            r_first(ph, s).start()
        for d in Z_NEAR:
            l_first(ph, d).start()

    def gather_relay(ph):
        for d in Z_NEAR:
            l_first(ph, d).wait_recv()
        for t in (1, 2, 0):
            l_second(ph, t).start()
        for s in range(4):
            r_first(ph, s).wait_recv()
        for i in (1, 2, 3):
            r_second(ph, i).start()

    def l_back(st, c):
        slot = 0 if c == 1 else 1 + k
        return send(ls.at[st, c - 1], lrecv.at[st, slot], as_.at[st, c - 1], ar.at[st, slot], sources[c - 1])

    def l_back_arrived(st, slot):
        return send(ls.at[st, 0], lrecv.at[st, slot], as_.at[st, 0], ar.at[st, slot], sources[0])

    def l_home(st, d):
        return send(lhs.at[st, d + 4], lh.at[st, d + 4], bs.at[st, d + 4], br.at[st, d + 4], at(x, y, z + d, k))

    def r_back(st, i):
        return send(rs.at[st, i], rrecv.at[st, i], cs.at[st, i], cr.at[st, i], at(x - X_STEP[i], y, z, k))

    def r_home(st, s):
        dy, dz = R_STEP[s]
        return send(rhs.at[st, s], rh.at[st, s], ds.at[st, s], dr.at[st, s], at(x, y + dy, z + dz, k))

    def pieces(v, left):
        norm = jnp.sum(v * v, axis=1, keepdims=True)
        hi = norm.astype(jnp.bfloat16).astype(jnp.float32)
        rest = norm - hi
        mid = rest.astype(jnp.bfloat16).astype(jnp.float32)
        low = rest - mid
        lane = lax.broadcasted_iota(jnp.int32, v.shape, 1)
        if left:
            p, q = (0, 3)
            scale, other = (1.0, 1.0)
        else:
            p, q = (3, 0)
            scale, other = (-0.5, -0.5)
        zero = jnp.zeros_like(v)
        out = jnp.where((lane >= q) & (lane < q + 3), other, zero)
        out = jnp.where(lane == p, scale * hi, out)
        out = jnp.where(lane == p + 1, scale * mid, out)
        return jnp.where(lane == p + 2, scale * low, out).astype(jnp.bfloat16)

    def prepare_left(st, c):
        rows = pl.ds(c * 512, 512)
        a = gl[st, c].reshape(512, 128)
        wide = a.astype(jnp.float32)
        la[rows, :] = pieces(wide, True)
        lat[0:128, rows] = wide.T.astype(jnp.bfloat16)

    def prepare_right(st, i):
        rows = pl.ds(i * 256, 256)
        b = gr[st, i].reshape(256, 128)
        wide = b.astype(jnp.float32)
        ra[rows, :] = pieces(wide, False)
        rt[:, rows] = wide.T

    ones = jnp.ones((512, 128), jnp.bfloat16)

    def produce(st, j, c, slot):
        rows, cols = pl.ds(c * 512, 512), pl.ds(j * 512, 512)
        a = gl[st, c].reshape(512, 128)
        b = gr[st, 2 * j : 2 * j + 2].reshape(512, 128)
        crossed = lax.dot_general(
            jnp.concatenate([a, la[rows, :]], axis=1), jnp.concatenate([b, ra[cols, :]], axis=1),
            LAST, preferred_element_type=jnp.float32,
        )
        if st == 0:
            weight = lax.dot_general(
                gl[2, c].reshape(512, 128), gr[2, 2 * j : 2 * j + 2].reshape(512, 128),
                LAST, preferred_element_type=jnp.float32,
            )
            kept[rows, cols] = weight.astype(jnp.bfloat16)
        else:
            weight = kept[rows, cols].astype(jnp.float32)
        prod[slot] = (weight * jnp.exp2(crossed * PAIR_SCALE)).astype(jnp.bfloat16)

    def consume(st, j, c, slot, first):
        rows = pl.ds(c * 512, 512)
        product = prod[slot]
        b = gr[st, 2 * j : 2 * j + 2].reshape(512, 128)
        left = jnp.dot(product, jnp.concatenate([b, ones], axis=1), preferred_element_type=jnp.float32)
        right = jnp.dot(lat[:, rows], product, preferred_element_type=jnp.float32)
        lacc[rows, :] = left if j == 0 else lacc[rows, :] + left
        racc[j] = right if first else racc[j] + right

    def left_term(st, c):
        rows = pl.ds(c * 512, 512)
        a = gl[st, c].reshape(512, 128).astype(jnp.float32)
        return lacc[rows, 0:128] - lacc[rows, 128:256] * a

    for st in range(STEPS):
        gather_start(st)
        if st == 0:
            gather_start(2)
        gather_relay(st)
        if st == 0:
            gather_relay(2)
        prepare_left(st, 0)
        prepare_right(st, 0)
        for c in (1, 2, 3):
            l_arrived(st, c).wait_recv()
            prepare_left(st, c)
        for i in (1, 2, 3):
            r_second(st, i).wait_recv()
            prepare_right(st, i)
        if st == 0:
            for c in (1, 2, 3):
                l_arrived(2, c).wait_recv()
            for i in (1, 2, 3):
                r_second(2, i).wait_recv()
        tiles = [(j, c) for j in range(2) for c in (2, 3, 1, 0)]
        produce(st, *tiles[0], 0)
        for t, (j, c) in enumerate(tiles):
            consume(st, j, c, t % 2, t % 4 == 0)
            if t < 7:
                produce(st, *tiles[t + 1], (t + 1) % 2)
            if j == 1 and c > 0:
                ls[st, c - 1] = left_term(st, c).astype(jnp.bfloat16)
                l_back(st, c).start()
            if t % 4 == 3:
                for i in (2 * j, 2 * j + 1):
                    cols, half = pl.ds(i * 256, 256), pl.ds((i % 2) * 256, 256)
                    term = racc[j, 0:128, half] - racc[j, 128:129, half] * rt[:, cols]
                    if i == 0:
                        rt[:, cols] = term
                    else:
                        rs[st, i] = term.astype(jnp.bfloat16)
                        r_back(st, i).start()
        for i in (1, 2, 3):
            r_back(st, i).wait_recv()
        total = rt[:, pl.ds(0, 256)]
        for i in (1, 2, 3):
            total = total + rrecv[st, i].astype(jnp.float32)
        rhs[st] = total.T.astype(jnp.bfloat16).reshape(4, 64, 128)
        for s in range(4):
            r_home(st, s).start()
        total = left_term(st, 0)
        for slot in range(3):
            l_back_arrived(st, slot).wait_recv()
            total = total + lrecv[st, slot].astype(jnp.float32)
        lhs[st] = total.astype(jnp.bfloat16).reshape(8, 64, 128)
        for d in Z_NEAR:
            l_home(st, d).start()
        left = lhs[st, 4].astype(jnp.float32)
        for d in Z_NEAR:
            l_home(st, d).wait_recv()
            left = left + lh[st, d + 4].astype(jnp.float32)
        left = left * GRAD_SCALE
        lv[...] = lv[...] - RATE * left
        right = jnp.zeros((64, 128), jnp.float32)
        for s in range(4):
            r_home(st, s).wait_recv()
            right = right + rh[st, s].astype(jnp.float32)
        right = right * GRAD_SCALE
        rv[...] = rv[...] - RATE * right
        if st + 1 < STEPS:
            gl[st + 1, 0, 4] = lv[...].astype(jnp.bfloat16)
            own_r[st + 1] = rv[...].astype(jnp.bfloat16)
        else:
            lf[...] = lv[...]
            rf[...] = rv[...]
            lg[...] = left
            rg[...] = right

    for ph in range(3):
        for d in Z_NEAR:
            l_first(ph, d).wait_send()
        for s in range(4):
            r_first(ph, s).wait_send()
        for t in range(3):
            l_second(ph, t).wait_send()
        for i in (1, 2, 3):
            r_second(ph, i).wait_send()
    for st in range(STEPS):
        for c in (1, 2, 3):
            l_back(st, c).wait_send()
        for d in Z_NEAR:
            l_home(st, d).wait_send()
        for i in (1, 2, 3):
            r_back(st, i).wait_send()
        for s in range(4):
            r_home(st, s).wait_send()


def body(left_points, right_points, left_cotangent, right_coefficient):
    f32, bf16 = jnp.float32, jnp.bfloat16
    dma = pltpu.SemaphoreType.DMA
    block = jax.ShapeDtypeStruct((64, 128), f32)
    return pl.pallas_call(
        pair_kernel,
        name="pairs",
        out_shape=(block,) * 4,
        in_specs=[pl.BlockSpec(memory_space=pl.ANY)] * 4,
        out_specs=[pl.BlockSpec(memory_space=pltpu.VMEM)] * 4,
        scratch_shapes=[
            pltpu.VMEM((64, 128), f32),
            pltpu.VMEM((64, 128), f32),
            pltpu.VMEM((3, 4, 8, 64, 128), bf16),
            pltpu.VMEM((3, 4, 4, 64, 128), bf16),
            pltpu.VMEM((3, 64, 128), bf16),
            pltpu.VMEM((2048, 128), bf16),
            pltpu.VMEM((144, 2048), bf16),
            pltpu.VMEM((1024, 128), bf16),
            pltpu.VMEM((128, 1024), f32),
            pltpu.VMEM((2, 512, 512), bf16),
            pltpu.VMEM((2048, 1024), bf16),
            pltpu.VMEM((2048, 256), f32),
            pltpu.VMEM((2, 144, 512), f32),
            pltpu.VMEM((2, 3, 512, 128), bf16),
            pltpu.VMEM((2, 3, 512, 128), bf16),
            pltpu.VMEM((2, 8, 64, 128), bf16),
            pltpu.VMEM((2, 8, 64, 128), bf16),
            pltpu.VMEM((2, 4, 128, 256), bf16),
            pltpu.VMEM((2, 4, 128, 256), bf16),
            pltpu.VMEM((2, 4, 64, 128), bf16),
            pltpu.VMEM((2, 4, 64, 128), bf16),
            dma((4,)),
            dma((3, 8)), dma((3, 8)),
            dma((3, 3)), dma((3, 3)),
            dma((3, 4)), dma((3, 4)),
            dma((3, 4)), dma((3, 4)),
            dma((2, 3)), dma((2, 3)),
            dma((2, 8)), dma((2, 8)),
            dma((2, 4)), dma((2, 4)),
            dma((2, 4)), dma((2, 4)),
        ],
        compiler_params=pltpu.CompilerParams(
            collective_id=0, has_side_effects=True, vmem_limit_bytes=48 * 2**20
        ),
    )(left_points, right_points, left_cotangent, right_coefficient)


def solution(mesh):
    spec = P(("row", "col"), None)
    return jax.shard_map(body, mesh=mesh, in_specs=(spec,) * 4, out_specs=(spec,) * 4, check_vma=False)
```

time: 428 us -> 91.1 us (0.21)
  waiting for transfers between devices: 198 us -> 0 us
  blocking collectives: 108 us -> 0 us
  Pallas kernels: 0 us -> 84.7 us
  starting transfers between devices: 68.8 us -> 0 us
  matrix products: 23.8 us -> 0 us
  between operations: 14.2 us -> 0.65 us
  other arithmetic: 5.85 us -> 0 us
    reduce_scatter x1 -> x0, waiting for transfers between devices: 111 us -> none  [body(): lax.psum_scatter(left_term, 'col', scatter_dimension=0, tiled=True)]
    all_to_all x6 -> x0, waiting for transfers between devices: 86.8 us -> none  [the longest x4 48.2 us: copy_for_each(): lax.all_to_all(jnp.broadcast_to(shard[None], (length, *shard.shape)), axi...]
    pallas_call x0 -> x1, Pallas kernels: none -> 84.7 us  [body(): pl.pallas_call(pair_kernel, name='pairs', out_shape=(block,) * 4, in_spec...]
    all_gather x1 -> x0, blocking collectives: 72.2 us -> none  [body(): left_panel = lax.all_gather(left_cotangent, 'col', axis=0, tiled=True)]
    all_to_all x6 -> x0, starting transfers between devices: 68.8 us -> none  [the longest x4 49.7 us: copy_for_each(): lax.all_to_all(jnp.broadcast_to(shard[None], (length, *shard.shape)), axi...]
    all_to_all x2 -> x0, blocking collectives: 35.5 us -> none  [the longest x1 18.3 us: copy_for_each(): lax.all_to_all(jnp.broadcast_to(shard[None], (length, *shard.shape)), axi...]
    dot_general x32 -> x0, matrix products: 23.8 us -> none  [the longest x8 9.26 us: visit_block(): jnp.dot(product, right_bf, preferred_element_type=jnp.float32)]
    unnamed x6 -> x12, local copies, waits for them, and re-layouts: 0.01 us -> 5.4 us
  transfers between devices with their start and end apart: 7 -> 0, of which waited for: 5 -> 0; matrix products, arithmetic and copies ran while one was open for 0% -> 0% of each run, Pallas kernels for 0% -> 0%
where the time goes in v1:
time: 91.1 us; the launch traced here: 90.7 us
  Pallas kernels  84.7 us (93%)
  local copies, waits for them, and re-layouts  5.4 us (6%)
    pallas_call x1, Pallas kernels, body(): pl.pallas_call(pair_kernel, name='pairs', out_shape=(block,) * 4, in_spec...  84.7 us
    unnamed x12, local copies, waits for them, and re-layouts  5.4 us

profile of v1, /device:TPU:1, one launch (start us, length us, event | category | flops | bytes accessed | tf_op | source)
XLA Modules:
  0.0 90.7 jit_solution(2185626675216464091)
XLA Ops:
  0.6 0.0 copy-start
  0.6 0.7 copy-done
  1.4 0.0 copy-start.1
  1.4 0.8 copy-done.1
  2.1 0.0 copy-start.2
  2.2 0.7 copy-done.2
  2.9 0.0 copy-start.3
  2.9 0.7 copy-done.3
  3.6 84.7 %pairs.1 = (f32[64,128]{1,0:T(8,128)S(1)}, f32[64,128]{1,0:T(8,128)S(1)}, f32[64,128]{1,0:T(8,128)S(1)}, f32[64,128]{1,0:T(8,128)S(1)}) custom-call(f32[64,128]{1,0:T(8,128)S(1)} %copy-done, f32[64,128]{1,0:T(8,128)S(1)} %copy-done.1, bf16[64,128]{1,0:T(8,128)(2,1)S(1)} %copy-done.2, bf16[64,128]{1,0:T(8,128)(2,1)S(1)} %copy-done.3), custom_call_target="tpu_custom_call" | custom-call | tf_op jit(solution)/shard_map/pairs/pallas_call | solution.py:280
  88.3 0.6 copy.12
  88.9 0.6 copy.13
  89.5 0.6 copy.14
  90.1 0.6 copy.15
Async XLA Ops:
  0.6 0.8 copy-start
  1.4 0.8 copy-start.1
  2.1 0.7 copy-start.2
  2.9 0.7 copy-start.3

commit v2 on v1

v2 whole, which is shorter than its diff:
```python
import jax
import jax.numpy as jnp
from jax import lax
from jax.experimental import pallas as pl
from jax.experimental.pallas import tpu as pltpu
from jax.sharding import PartitionSpec as P

STEPS = 2
PAIR_SCALE = 0.0625 * 1.4426950408889634
GRAD_SCALE = 0.0625
RATE = 0.3
MESH = pl.DeviceIdType.MESH
LAST = (((1,), (1,)), ((), ()))

Z_LEFT = (-1, 0, 1, 2)
Z_RIGHT = ((-6, 6), (-2, 2))


def pair_kernel(lp, rp, lc, rc, lf, rf, lg, rg, lv, rv, gl, gr, own_r, la, lat, ra, rt, prod, kept, lacc, racc,
                ss, ssr, sx, sxr, sz, szr, ty, tyr, tz, tzr,
                in_sem, lz_s, lz_r, lx_s, lx_r, lk_s, lk_r, rz_s, rz_r, ry_s, ry_r,
                bk_s, bk_r, bx_s, bx_r, bz_s, bz_r, cy_s, cy_r, cz_s, cz_r):
    row, col = lax.axis_index("row"), lax.axis_index("col")
    x, k = row % 4, col % 2
    y = (col // 2) % 4
    z = (col // 8) * 4 + row // 4
    way = 1 - 2 * k

    def at(dx=0, dy=0, dz=0, core=None):
        px, py, pz = (x + dx + 4) % 4, (y + dy + 4) % 4, (z + dz + 16) % 16
        return ((pz % 4) * 4 + px, (pz // 4) * 8 + py * 2 + (k if core is None else core))

    sibling = at(core=1 - k)
    at_x = [None] + [at(dx=i) for i in (1, 2, 3)]
    at_y = [None] + [at(dy=i) for i in (1, 2, 3)]
    z_up = [at(dz=way * o) for o in Z_LEFT]
    z_down = [at(dz=-way * o) for o in Z_LEFT]
    z_far = {o: at(dz=o) for o in (-6, -2, 2, 6)}

    barrier = pltpu.get_barrier_semaphore()
    partners = [z_far[-6], z_far[6], z_far[-2], z_far[2], at(dz=1), at(dz=-1), *at_x[1:], *at_y[1:], sibling]
    for p in partners:
        pl.semaphore_signal(barrier, inc=1, device_id=p, device_id_type=MESH)

    loads = [
        pltpu.make_async_copy(lp, lv, in_sem.at[0]),
        pltpu.make_async_copy(rp, rv, in_sem.at[1]),
        pltpu.make_async_copy(lc, gl.at[2, 0, 0, 1], in_sem.at[2]),
        pltpu.make_async_copy(rc, own_r.at[2], in_sem.at[3]),
    ]
    for c in loads:
        c.start()
    lat[128:144, :] = jnp.ones((16, 2048), jnp.bfloat16)
    for c in loads:
        c.wait()
    gl[0, 0, 0, 1] = lv[...].astype(jnp.bfloat16)
    own_r[0] = rv[...].astype(jnp.bfloat16)
    pl.semaphore_wait(barrier, len(partners))

    def send(src, dst, s, r, device):
        return pltpu.make_async_remote_copy(
            src_ref=src, dst_ref=dst, send_sem=s, recv_sem=r, device_id=device, device_id_type=MESH
        )

    pending = []

    def go(copy):
        copy.start()
        pending.append(copy)

    def l_z(ph, i):
        return send(gl.at[ph, 0, 0, 1], gl.at[ph, 0, 0, i], lz_s.at[ph, i], lz_r.at[ph, i], z_down[i])

    def l_x(ph, i):
        return send(gl.at[ph, 0, 0], gl.at[ph, 0, i], lx_s.at[ph, i], lx_r.at[ph, i], at_x[i])

    def l_k(ph, i):
        return send(gl.at[ph, 0, i], gl.at[ph, 1, i], lk_s.at[ph, i], lk_r.at[ph, i], sibling)

    def r_z(ph, h, s):
        n = 2 * h + s
        return send(own_r.at[ph], gr.at[ph, h, 0, s], rz_s.at[ph, n], rz_r.at[ph, n], z_far[-Z_RIGHT[h][s]])

    def r_y(ph, h, i):
        n = 4 * h + i
        return send(gr.at[ph, h, 0], gr.at[ph, h, i], ry_s.at[ph, n], ry_r.at[ph, n], at_y[i])

    def gather_start(ph):
        go(r_z(ph, 0, 0))
        go(r_z(ph, 0, 1))
        for i in (3, 0, 2):
            go(l_z(ph, i))
        go(r_z(ph, 1, 0))
        go(r_z(ph, 1, 1))

    def relay_left(ph):
        for i in (0, 2, 3):
            l_z(ph, i).wait_recv()
        for i in (2, 1, 3):
            go(l_x(ph, i))
        go(l_k(ph, 0))

    def relay_right(ph, h):
        r_z(ph, h, 0).wait_recv()
        r_z(ph, h, 1).wait_recv()
        for i in (2, 1, 3):
            go(r_y(ph, h, i))

    def relay_sibling(ph):
        for i in (1, 3, 2):
            l_x(ph, i).wait_recv()
            go(l_k(ph, i))

    def b_k(st, c):
        return send(ss.at[st, c], ssr.at[st, c], bk_s.at[st, c], bk_r.at[st, c], sibling)

    def b_x(st, i):
        return send(sx.at[st, i], sxr.at[st, i], bx_s.at[st, i], bx_r.at[st, i], at_x[4 - i])

    def b_z(st, i):
        return send(sz.at[st, i], szr.at[st, i], bz_s.at[st, i], bz_r.at[st, i], z_up[i])

    def c_y(st, h, i):
        n = 4 * h + i
        return send(ty.at[st, h, i], tyr.at[st, h, i], cy_s.at[st, n], cy_r.at[st, n], at_y[4 - i])

    def c_z(st, h, s):
        n = 2 * h + s
        return send(tz.at[st, n], tzr.at[st, n], cz_s.at[st, n], cz_r.at[st, n], z_far[Z_RIGHT[h][s]])

    def pieces(v, own, other, scale):
        norm = jnp.sum(v * v, axis=1, keepdims=True)
        hi = norm.astype(jnp.bfloat16).astype(jnp.float32)
        rest = norm - hi
        mid = rest.astype(jnp.bfloat16).astype(jnp.float32)
        low = rest - mid
        lane = lax.broadcasted_iota(jnp.int32, v.shape, 1)
        out = jnp.where((lane >= other) & (lane < other + 3), scale, jnp.zeros_like(v))
        out = jnp.where(lane == own, scale * hi, out)
        out = jnp.where(lane == own + 1, scale * mid, out)
        return jnp.where(lane == own + 2, scale * low, out).astype(jnp.bfloat16)

    def prepare_left(st, m, i):
        rows = pl.ds((4 * m + i) * 256, 256)
        wide = gl[st, m, i].reshape(256, 128).astype(jnp.float32)
        la[rows, :] = pieces(wide, 0, 3, 1.0)
        lat[0:128, rows] = wide.T.astype(jnp.bfloat16)

    def prepare_right(st, h, i):
        rows = pl.ds((4 * h + i) * 128, 128)
        wide = gr[st, h, i].reshape(128, 128).astype(jnp.float32)
        ra[rows, :] = pieces(wide, 3, 0, -0.5)
        rt[:, rows] = wide.T

    ones = jnp.ones((512, 128), jnp.bfloat16)

    def lefts(ph, c):
        return gl[ph, c // 2, 2 * (c % 2) : 2 * (c % 2) + 2].reshape(512, 128)

    def produce(st, h, c, slot):
        rows, cols = pl.ds(c * 512, 512), pl.ds(h * 512, 512)
        crossed = lax.dot_general(
            jnp.concatenate([lefts(st, c), la[rows, :]], axis=1),
            jnp.concatenate([gr[st, h].reshape(512, 128), ra[cols, :]], axis=1),
            LAST, preferred_element_type=jnp.float32,
        )
        if st == 0:
            weight = lax.dot_general(
                lefts(2, c), gr[2, h].reshape(512, 128), LAST, preferred_element_type=jnp.float32
            )
            kept[rows, cols] = weight.astype(jnp.bfloat16)
        else:
            weight = kept[rows, cols].astype(jnp.float32)
        prod[slot] = (weight * jnp.exp2(crossed * PAIR_SCALE)).astype(jnp.bfloat16)

    def consume(st, h, c, slot, first_h, first_c):
        rows = pl.ds(c * 512, 512)
        product = prod[slot]
        b = gr[st, h].reshape(512, 128)
        left = jnp.dot(product, jnp.concatenate([b, ones], axis=1), preferred_element_type=jnp.float32)
        right = jnp.dot(lat[:, rows], product, preferred_element_type=jnp.float32)
        lacc[rows, :] = left if first_h else lacc[rows, :] + left
        racc[h] = right if first_c else racc[h] + right

    def left_term(st, c):
        rows = pl.ds(c * 512, 512)
        return lacc[rows, 0:128] - lacc[rows, 128:256] * lefts(st, c).astype(jnp.float32)

    def right_out(st, h):
        term = racc[h, 0:128, :] - racc[h, 128:129, :] * rt[:, pl.ds(h * 512, 512)]
        rt[:, pl.ds(h * 512, 128)] = term[:, 0:128]
        for i in (2, 1, 3):
            ty[st, h, i] = term[:, 128 * i : 128 * i + 128].astype(jnp.bfloat16)
            go(c_y(st, h, i))

    def right_home(st, h):
        total = rt[:, pl.ds(h * 512, 128)]
        for i in (1, 3, 2):
            c_y(st, h, i).wait_recv()
            total = total + tyr[st, h, i].astype(jnp.float32)
        tz[st, 2 * h : 2 * h + 2] = total.T.astype(jnp.bfloat16).reshape(2, 64, 128)
        go(c_z(st, h, 0))
        go(c_z(st, h, 1))

    for st in range(STEPS):
        gather_start(st)
        if st == 0:
            gather_start(2)
        relay_left(st)
        relay_right(st, 1)
        prepare_left(st, 0, 0)
        relay_right(st, 0)
        if st == 0:
            relay_left(2)
            relay_right(2, 1)
            relay_right(2, 0)
        relay_sibling(st)
        for i in (1, 2, 3):
            prepare_left(st, 0, i)
        for h in (1, 0):
            for i in range(4):
                if i:
                    r_y(st, h, i).wait_recv()
                prepare_right(st, h, i)
        if st == 0:
            relay_sibling(2)
        for i in range(4):
            l_k(st, i).wait_recv()
            prepare_left(st, 1, i)
        if st == 0:
            for h in range(2):
                for i in (1, 2, 3):
                    r_y(2, h, i).wait_recv()
            for i in range(4):
                l_k(2, i).wait_recv()

        tiles = [(0, c) for c in (0, 1, 2, 3)] + [(1, c) for c in (3, 2, 1, 0)]
        produce(st, *tiles[0], 0)
        for t, (h, c) in enumerate(tiles):
            consume(st, h, c, t % 2, h == 0, t % 4 == 0)
            if t < 7:
                produce(st, *tiles[t + 1], (t + 1) % 2)
            if t == 3:
                right_out(st, 0)
            if h == 1 and c >= 2:
                ss[st, c - 2] = left_term(st, c).astype(jnp.bfloat16)
                go(b_k(st, c - 2))
            if h == 1 and c == 1:
                b_k(st, 1).wait_recv()
                total = left_term(st, 1) + ssr[st, 1].astype(jnp.float32)
                sx[st, 2:4] = total.astype(jnp.bfloat16).reshape(2, 256, 128)
                go(b_x(st, 2))
                go(b_x(st, 3))
        b_k(st, 0).wait_recv()
        total = left_term(st, 0) + ssr[st, 0].astype(jnp.float32)
        sx[st, 1] = total[256:512].astype(jnp.bfloat16)
        go(b_x(st, 1))
        right_out(st, 1)
        right_home(st, 0)
        total = total[0:256]
        for i in (3, 2, 1):
            b_x(st, i).wait_recv()
            total = total + sxr[st, i].astype(jnp.float32)
        sz[st] = total.astype(jnp.bfloat16).reshape(4, 64, 128)
        for i in (3, 0, 2):
            go(b_z(st, i))
        left = total[64:128]
        right_home(st, 1)
        for i in (0, 2, 3):
            b_z(st, i).wait_recv()
            left = left + szr[st, i].astype(jnp.float32)
        left = left * GRAD_SCALE
        lv[...] = lv[...] - RATE * left
        if st + 1 < STEPS:
            gl[st + 1, 0, 0, 1] = lv[...].astype(jnp.bfloat16)
        right = jnp.zeros((64, 128), jnp.float32)
        for h in (1, 0):
            for s in range(2):
                c_z(st, h, s).wait_recv()
                right = right + tzr[st, 2 * h + s].astype(jnp.float32)
        right = right * GRAD_SCALE
        rv[...] = rv[...] - RATE * right
        if st + 1 < STEPS:
            own_r[st + 1] = rv[...].astype(jnp.bfloat16)
        else:
            lf[...] = lv[...]
            rf[...] = rv[...]
            lg[...] = left
            rg[...] = right

    for copy in pending:
        copy.wait_send()


def body(left_points, right_points, left_cotangent, right_coefficient):
    f32, bf16 = jnp.float32, jnp.bfloat16
    dma = pltpu.SemaphoreType.DMA
    block = jax.ShapeDtypeStruct((64, 128), f32)
    return pl.pallas_call(
        pair_kernel,
        name="pairs",
        out_shape=(block,) * 4,
        in_specs=[pl.BlockSpec(memory_space=pl.ANY)] * 4,
        out_specs=[pl.BlockSpec(memory_space=pltpu.VMEM)] * 4,
        scratch_shapes=[
            pltpu.VMEM((64, 128), f32),
            pltpu.VMEM((64, 128), f32),
            pltpu.VMEM((3, 2, 4, 4, 64, 128), bf16),
            pltpu.VMEM((3, 2, 4, 2, 64, 128), bf16),
            pltpu.VMEM((3, 64, 128), bf16),
            pltpu.VMEM((2048, 128), bf16),
            pltpu.VMEM((144, 2048), bf16),
            pltpu.VMEM((1024, 128), bf16),
            pltpu.VMEM((128, 1024), f32),
            pltpu.VMEM((2, 512, 512), bf16),
            pltpu.VMEM((2048, 1024), bf16),
            pltpu.VMEM((2048, 256), f32),
            pltpu.VMEM((2, 144, 512), f32),
            pltpu.VMEM((2, 2, 512, 128), bf16),
            pltpu.VMEM((2, 2, 512, 128), bf16),
            pltpu.VMEM((2, 4, 256, 128), bf16),
            pltpu.VMEM((2, 4, 256, 128), bf16),
            pltpu.VMEM((2, 4, 64, 128), bf16),
            pltpu.VMEM((2, 4, 64, 128), bf16),
            pltpu.VMEM((2, 2, 4, 128, 128), bf16),
            pltpu.VMEM((2, 2, 4, 128, 128), bf16),
            pltpu.VMEM((2, 4, 64, 128), bf16),
            pltpu.VMEM((2, 4, 64, 128), bf16),
            dma((4,)),
            dma((3, 4)), dma((3, 4)),
            dma((3, 4)), dma((3, 4)),
            dma((3, 4)), dma((3, 4)),
            dma((3, 4)), dma((3, 4)),
            dma((3, 8)), dma((3, 8)),
            dma((2, 2)), dma((2, 2)),
            dma((2, 4)), dma((2, 4)),
            dma((2, 4)), dma((2, 4)),
            dma((2, 8)), dma((2, 8)),
            dma((2, 4)), dma((2, 4)),
        ],
        compiler_params=pltpu.CompilerParams(
            collective_id=0, has_side_effects=True, vmem_limit_bytes=64 * 2**20 - 2**16
        ),
    )(left_points, right_points, left_cotangent, right_coefficient)


def solution(mesh):
    spec = P(("row", "col"), None)
    return jax.shard_map(body, mesh=mesh, in_specs=(spec,) * 4, out_specs=(spec,) * 4, check_vma=False)
```

time: 91.1 us -> 77.7 us (0.85)
  Pallas kernels: 84.7 us -> 73.1 us
  local copies, waits for them, and re-layouts: 5.4 us -> 3.54 us
    pallas_call x1, Pallas kernels: 84.7 us -> 73.1 us  [body(): pl.pallas_call(pair_kernel, name='pairs', out_shape=(block,) * 4, in_spec...]
    unnamed x12 -> x10, local copies, waits for them, and re-layouts: 5.4 us -> 3.54 us
where the time goes in v2:
time: 77.7 us; the launch traced here: 77.3 us
  Pallas kernels  73.1 us (94%)
  local copies, waits for them, and re-layouts  3.54 us (5%)
    pallas_call x1, Pallas kernels, body(): pl.pallas_call(pair_kernel, name='pairs', out_shape=(block,) * 4, in_spec...  73.1 us
    unnamed x10, local copies, waits for them, and re-layouts  3.54 us

profile of v2, /device:TPU:1, one launch (start us, length us, event | category | flops | bytes accessed | tf_op | source)
XLA Modules:
  0.0 77.3 jit_solution(11259525274081300582)
XLA Ops:
  0.6 73.1 %pairs.1 = (f32[64,128]{1,0:T(8,128)}, f32[64,128]{1,0:T(8,128)}, f32[64,128]{1,0:T(8,128)}, f32[64,128]{1,0:T(8,128)}) custom-call(f32[64,128]{1,0:T(8,128)} %lp.1, f32[64,128]{1,0:T(8,128)} %rp.1, bf16[64,128]{1,0:T(8,128)(2,1)} %lc.1, bf16[64,128]{1,0:T(8,128)(2,1)} %rc.1), custom_call_target="tpu_custom_call" | custom-call | tf_op jit(solution)/shard_map/pairs/pallas_call | solution.py:299
  73.7 0.0 copy-start.2
  73.7 1.4 %copy.12 = f32[64,128]{1,0:T(8,128)} copy(f32[64,128]{1,0:T(8,128)} %get-tuple-element.8) | data formatting | bytes 65536
  75.1 0.0 copy-done.2
  75.1 0.0 copy-start.1
  75.1 0.6 copy.13
  75.7 0.2 copy-done.1
  75.9 0.0 copy-start
  75.9 0.6 copy.14
  76.5 0.2 copy-done
  76.7 0.6 copy.15
Async XLA Ops:
  73.7 1.4 %copy-start.2 = (f32[64,128]{1,0:T(8,128)S(1)}, f32[64,128]{1,0:T(8,128)}, u32[]{:S(2)}) copy-start(f32[64,128]{1,0:T(8,128)} %get-tuple-element.9) | copy-start | bytes 98308
  75.1 0.8 copy-start.1
  75.9 0.8 copy-start

commit v3 on v2

--- a/solution.py
+++ b/solution.py
@@ -16,7 +16,7 @@
 Z_RIGHT = ((-6, 6), (-2, 2))
 
 
-def pair_kernel(lp, rp, lc, rc, lf, rf, lg, rg, lv, rv, gl, gr, own_r, la, lat, ra, rt, prod, kept, lacc, racc,
+def pair_kernel(lp, rp, lc, rc, result, lv, rv, gl, gr, own_r, la, lat, ra, rt, prod, kept, lacc, racc,
                 ss, ssr, sx, sxr, sz, szr, ty, tyr, tz, tzr,
                 in_sem, lz_s, lz_r, lx_s, lx_r, lk_s, lk_r, rz_s, rz_r, ry_s, ry_r,
                 bk_s, bk_r, bx_s, bx_r, bz_s, bz_r, cy_s, cy_r, cz_s, cz_r):
@@ -68,6 +68,11 @@
         copy.start()
         pending.append(copy)
 
+    def sent(keep):
+        for copy in pending[: len(pending) - keep]:
+            copy.wait_send()
+        del pending[: len(pending) - keep]
+
     def l_z(ph, i):
         return send(gl.at[ph, 0, 0, 1], gl.at[ph, 0, 0, i], lz_s.at[ph, i], lz_r.at[ph, i], z_down[i])
 
@@ -157,21 +162,25 @@
     def lefts(ph, c):
         return gl[ph, c // 2, 2 * (c % 2) : 2 * (c % 2) + 2].reshape(512, 128)
 
-    def produce(st, h, c, slot):
+    def factor(st, h, c):
         rows, cols = pl.ds(c * 512, 512), pl.ds(h * 512, 512)
         crossed = lax.dot_general(
             jnp.concatenate([lefts(st, c), la[rows, :]], axis=1),
             jnp.concatenate([gr[st, h].reshape(512, 128), ra[cols, :]], axis=1),
             LAST, preferred_element_type=jnp.float32,
         )
+        return jnp.exp2(crossed * PAIR_SCALE)
+
+    def produce(st, h, c, slot):
+        rows, cols = pl.ds(c * 512, 512), pl.ds(h * 512, 512)
         if st == 0:
             weight = lax.dot_general(
                 lefts(2, c), gr[2, h].reshape(512, 128), LAST, preferred_element_type=jnp.float32
             )
+            prod[slot] = (weight * kept[rows, cols].astype(jnp.float32)).astype(jnp.bfloat16)
             kept[rows, cols] = weight.astype(jnp.bfloat16)
         else:
-            weight = kept[rows, cols].astype(jnp.float32)
-        prod[slot] = (weight * jnp.exp2(crossed * PAIR_SCALE)).astype(jnp.bfloat16)
+            prod[slot] = (kept[rows, cols].astype(jnp.float32) * factor(st, h, c)).astype(jnp.bfloat16)
 
     def consume(st, h, c, slot, first_h, first_c):
         rows = pl.ds(c * 512, 512)
@@ -206,6 +215,8 @@
         gather_start(st)
         if st == 0:
             gather_start(2)
+        else:
+            sent(7)
         relay_left(st)
         relay_right(st, 1)
         prepare_left(st, 0, 0)
@@ -228,6 +239,9 @@
             l_k(st, i).wait_recv()
             prepare_left(st, 1, i)
         if st == 0:
+            for h in range(2):
+                for c in range(4):
+                    kept[pl.ds(c * 512, 512), pl.ds(h * 512, 512)] = factor(0, h, c).astype(jnp.bfloat16)
             for h in range(2):
                 for i in (1, 2, 3):
                     r_y(2, h, i).wait_recv()
@@ -266,42 +280,41 @@
             go(b_z(st, i))
         left = total[64:128]
         right_home(st, 1)
+        if st + 1 == STEPS:
+            sent(5)
         for i in (0, 2, 3):
             b_z(st, i).wait_recv()
             left = left + szr[st, i].astype(jnp.float32)
-        left = left * GRAD_SCALE
-        lv[...] = lv[...] - RATE * left
         if st + 1 < STEPS:
+            lv[...] = lv[...] - RATE * (left * GRAD_SCALE)
             gl[st + 1, 0, 0, 1] = lv[...].astype(jnp.bfloat16)
         right = jnp.zeros((64, 128), jnp.float32)
         for h in (1, 0):
             for s in range(2):
                 c_z(st, h, s).wait_recv()
                 right = right + tzr[st, 2 * h + s].astype(jnp.float32)
-        right = right * GRAD_SCALE
-        rv[...] = rv[...] - RATE * right
         if st + 1 < STEPS:
+            rv[...] = rv[...] - RATE * (right * GRAD_SCALE)
             own_r[st + 1] = rv[...].astype(jnp.bfloat16)
         else:
-            lf[...] = lv[...]
-            rf[...] = rv[...]
-            lg[...] = left
-            rg[...] = right
-
-    for copy in pending:
-        copy.wait_send()
+            left, right = left * GRAD_SCALE, right * GRAD_SCALE
+            result[0:64, :] = lv[...] - RATE * left
+            result[64:128, :] = rv[...] - RATE * right
+            result[128:192, :] = left
+            result[192:256, :] = right
+
+    sent(0)
 
 
 def body(left_points, right_points, left_cotangent, right_coefficient):
     f32, bf16 = jnp.float32, jnp.bfloat16
     dma = pltpu.SemaphoreType.DMA
-    block = jax.ShapeDtypeStruct((64, 128), f32)
-    return pl.pallas_call(
+    result = pl.pallas_call(
         pair_kernel,
         name="pairs",
-        out_shape=(block,) * 4,
+        out_shape=jax.ShapeDtypeStruct((256, 128), f32),
         in_specs=[pl.BlockSpec(memory_space=pl.ANY)] * 4,
-        out_specs=[pl.BlockSpec(memory_space=pltpu.VMEM)] * 4,
+        out_specs=pl.BlockSpec(memory_space=pltpu.VMEM),
         scratch_shapes=[
             pltpu.VMEM((64, 128), f32),
             pltpu.VMEM((64, 128), f32),
@@ -342,6 +355,7 @@
             collective_id=0, has_side_effects=True, vmem_limit_bytes=64 * 2**20 - 2**16
         ),
     )(left_points, right_points, left_cotangent, right_coefficient)
+    return tuple(result[64 * i : 64 * i + 64] for i in range(4))
 
 
 def solution(mesh):

time: 77.7 us -> 73.7 us (0.949)
  local copies, waits for them, and re-layouts: 3.54 us -> 1.46 us
  Pallas kernels: 73.1 us -> 71.3 us
    unnamed x10 -> x0, local copies, waits for them, and re-layouts: 3.54 us -> none
    pallas_call x1, Pallas kernels: 73.1 us -> 71.3 us  [body(): pl.pallas_call(pair_kernel, name='pairs', out_shape=jax.ShapeDtypeStruct(...]
    slice x0 -> x1, local copies, waits for them, and re-layouts: none -> 1.46 us  [body(): return tuple((result[64 * i:64 * i + 64] for i in range(4)))]
where the time goes in v3:
time: 73.7 us; the launch traced here: 73.4 us
  Pallas kernels  71.3 us (97%)
  local copies, waits for them, and re-layouts  1.46 us (2%)
    pallas_call x1, Pallas kernels, body(): pl.pallas_call(pair_kernel, name='pairs', out_shape=jax.ShapeDtypeStruct(...  71.3 us

profile of v3, /device:TPU:1, one launch (start us, length us, event | category | flops | bytes accessed | tf_op | source)
XLA Modules:
  0.0 73.4 jit_solution(4664688730428349032)
XLA Ops:
  0.6 71.3 %pairs.1 = f32[256,128]{1,0:T(8,128)} custom-call(f32[64,128]{1,0:T(8,128)} %lp.1, f32[64,128]{1,0:T(8,128)} %rp.1, bf16[64,128]{1,0:T(8,128)(2,1)} %lc.1, bf16[64,128]{1,0:T(8,128)(2,1)} %rc.1), custom_call_target="tpu_custom_call" | custom-call | tf_op jit(solution)/shard_map/pairs/pallas_call | solution.py:312
  72.0 1.5 %fusion = (f32[64,128]{1,0:T(8,128)}, f32[64,128]{1,0:T(8,128)}, f32[64,128]{1,0:T(8,128)}, f32[64,128]{1,0:T(8,128)}) fusion(f32[256,128]{1,0:T(8,128)} %pairs.1), kind=kLoop, calls=%fused_computation | loop fusion | bytes 262144 | tf_op jit(solution)/shard_map/slice | solution.py:358

commit v4 on v3

--- a/solution.py
+++ b/solution.py
@@ -12,11 +12,11 @@
 MESH = pl.DeviceIdType.MESH
 LAST = (((1,), (1,)), ((), ()))
 
-Z_LEFT = (-1, 0, 1, 2)
-Z_RIGHT = ((-6, 6), (-2, 2))
-
-
-def pair_kernel(lp, rp, lc, rc, result, lv, rv, gl, gr, own_r, la, lat, ra, rt, prod, kept, lacc, racc,
+Z_LEFT = (-3, -1, 1, 3)
+Z_RIGHT = ((5, -4), (-3, 4))
+
+
+def pair_kernel(lp, rp, lc, rc, result, lv, rv, gl, gr, own_l, own_r, la, lat, ra, rt, prod, kept, lacc, racc,
                 ss, ssr, sx, sxr, sz, szr, ty, tyr, tz, tzr,
                 in_sem, lz_s, lz_r, lx_s, lx_r, lk_s, lk_r, rz_s, rz_r, ry_s, ry_r,
                 bk_s, bk_r, bx_s, bx_r, bz_s, bz_r, cy_s, cy_r, cz_s, cz_r):
@@ -33,19 +33,18 @@
     sibling = at(core=1 - k)
     at_x = [None] + [at(dx=i) for i in (1, 2, 3)]
     at_y = [None] + [at(dy=i) for i in (1, 2, 3)]
-    z_up = [at(dz=way * o) for o in Z_LEFT]
-    z_down = [at(dz=-way * o) for o in Z_LEFT]
-    z_far = {o: at(dz=o) for o in (-6, -2, 2, 6)}
+    z_left = {o: at(dz=o) for o in Z_LEFT}
+    z_right = {o: at(dz=way * o) for o in (-5, -4, -3, 3, 4, 5)}
 
     barrier = pltpu.get_barrier_semaphore()
-    partners = [z_far[-6], z_far[6], z_far[-2], z_far[2], at(dz=1), at(dz=-1), *at_x[1:], *at_y[1:], sibling]
+    partners = [*z_left.values(), z_right[-4], z_right[4], z_right[-5], z_right[5], *at_x[1:], *at_y[1:], sibling]
     for p in partners:
         pl.semaphore_signal(barrier, inc=1, device_id=p, device_id_type=MESH)
 
     loads = [
         pltpu.make_async_copy(lp, lv, in_sem.at[0]),
         pltpu.make_async_copy(rp, rv, in_sem.at[1]),
-        pltpu.make_async_copy(lc, gl.at[2, 0, 0, 1], in_sem.at[2]),
+        pltpu.make_async_copy(lc, own_l.at[2], in_sem.at[2]),
         pltpu.make_async_copy(rc, own_r.at[2], in_sem.at[3]),
     ]
     for c in loads:
@@ -53,7 +52,7 @@
     lat[128:144, :] = jnp.ones((16, 2048), jnp.bfloat16)
     for c in loads:
         c.wait()
-    gl[0, 0, 0, 1] = lv[...].astype(jnp.bfloat16)
+    own_l[0] = lv[...].astype(jnp.bfloat16)
     own_r[0] = rv[...].astype(jnp.bfloat16)
     pl.semaphore_wait(barrier, len(partners))
 
@@ -74,7 +73,7 @@
         del pending[: len(pending) - keep]
 
     def l_z(ph, i):
-        return send(gl.at[ph, 0, 0, 1], gl.at[ph, 0, 0, i], lz_s.at[ph, i], lz_r.at[ph, i], z_down[i])
+        return send(own_l.at[ph], gl.at[ph, 0, 0, i], lz_s.at[ph, i], lz_r.at[ph, i], z_left[-Z_LEFT[i]])
 
     def l_x(ph, i):
         return send(gl.at[ph, 0, 0], gl.at[ph, 0, i], lx_s.at[ph, i], lx_r.at[ph, i], at_x[i])
@@ -84,22 +83,22 @@
 
     def r_z(ph, h, s):
         n = 2 * h + s
-        return send(own_r.at[ph], gr.at[ph, h, 0, s], rz_s.at[ph, n], rz_r.at[ph, n], z_far[-Z_RIGHT[h][s]])
+        return send(own_r.at[ph], gr.at[ph, h, 0, s], rz_s.at[ph, n], rz_r.at[ph, n], z_right[-Z_RIGHT[h][s]])
 
     def r_y(ph, h, i):
         n = 4 * h + i
         return send(gr.at[ph, h, 0], gr.at[ph, h, i], ry_s.at[ph, n], ry_r.at[ph, n], at_y[i])
 
-    def gather_start(ph):
-        go(r_z(ph, 0, 0))
-        go(r_z(ph, 0, 1))
-        for i in (3, 0, 2):
+    def start_left(ph):
+        for i in (0, 3, 1, 2):
             go(l_z(ph, i))
-        go(r_z(ph, 1, 0))
-        go(r_z(ph, 1, 1))
+
+    def start_right(ph, h):
+        go(r_z(ph, h, 0))
+        go(r_z(ph, h, 1))
 
     def relay_left(ph):
-        for i in (0, 2, 3):
+        for i in (1, 2, 0, 3):
             l_z(ph, i).wait_recv()
         for i in (2, 1, 3):
             go(l_x(ph, i))
@@ -123,7 +122,7 @@
         return send(sx.at[st, i], sxr.at[st, i], bx_s.at[st, i], bx_r.at[st, i], at_x[4 - i])
 
     def b_z(st, i):
-        return send(sz.at[st, i], szr.at[st, i], bz_s.at[st, i], bz_r.at[st, i], z_up[i])
+        return send(sz.at[st, i], szr.at[st, i], bz_s.at[st, i], bz_r.at[st, i], z_left[Z_LEFT[i]])
 
     def c_y(st, h, i):
         n = 4 * h + i
@@ -131,7 +130,7 @@
 
     def c_z(st, h, s):
         n = 2 * h + s
-        return send(tz.at[st, n], tzr.at[st, n], cz_s.at[st, n], cz_r.at[st, n], z_far[Z_RIGHT[h][s]])
+        return send(tz.at[st, n], tzr.at[st, n], cz_s.at[st, n], cz_r.at[st, n], z_right[Z_RIGHT[h][s]])
 
     def pieces(v, own, other, scale):
         norm = jnp.sum(v * v, axis=1, keepdims=True)
@@ -157,6 +156,12 @@
         ra[rows, :] = pieces(wide, 3, 0, -0.5)
         rt[:, rows] = wide.T
 
+    def right_arrived(st, h):
+        for i in (0, 1, 3, 2):
+            if i:
+                r_y(st, h, i).wait_recv()
+            prepare_right(st, h, i)
+
     ones = jnp.ones((512, 128), jnp.bfloat16)
 
     def lefts(ph, c):
@@ -212,11 +217,16 @@
         go(c_z(st, h, 1))
 
     for st in range(STEPS):
-        gather_start(st)
-        if st == 0:
-            gather_start(2)
+        start_right(st, 0)
+        if st == 0:
+            start_left(st)
+        start_right(st, 1)
+        if st == 0:
+            start_right(2, 0)
+            start_left(2)
+            start_right(2, 1)
         else:
-            sent(7)
+            sent(8)
         relay_left(st)
         relay_right(st, 1)
         prepare_left(st, 0, 0)
@@ -228,18 +238,15 @@
         relay_sibling(st)
         for i in (1, 2, 3):
             prepare_left(st, 0, i)
-        for h in (1, 0):
-            for i in range(4):
-                if i:
-                    r_y(st, h, i).wait_recv()
-                prepare_right(st, h, i)
-        if st == 0:
-            relay_sibling(2)
+        right_arrived(st, 1)
         for i in range(4):
             l_k(st, i).wait_recv()
             prepare_left(st, 1, i)
+        right_arrived(st, 0)
         if st == 0:
             for h in range(2):
+                if h == 1:
+                    relay_sibling(2)
                 for c in range(4):
                     kept[pl.ds(c * 512, 512), pl.ds(h * 512, 512)] = factor(0, h, c).astype(jnp.bfloat16)
             for h in range(2):
@@ -276,18 +283,19 @@
             b_x(st, i).wait_recv()
             total = total + sxr[st, i].astype(jnp.float32)
         sz[st] = total.astype(jnp.bfloat16).reshape(4, 64, 128)
-        for i in (3, 0, 2):
+        for i in (0, 3, 1, 2):
             go(b_z(st, i))
-        left = total[64:128]
+        left = jnp.zeros((64, 128), jnp.float32)
         right_home(st, 1)
         if st + 1 == STEPS:
-            sent(5)
-        for i in (0, 2, 3):
+            sent(6)
+        for i in (1, 2, 0, 3):
             b_z(st, i).wait_recv()
             left = left + szr[st, i].astype(jnp.float32)
         if st + 1 < STEPS:
             lv[...] = lv[...] - RATE * (left * GRAD_SCALE)
-            gl[st + 1, 0, 0, 1] = lv[...].astype(jnp.bfloat16)
+            own_l[st + 1] = lv[...].astype(jnp.bfloat16)
+            start_left(st + 1)
         right = jnp.zeros((64, 128), jnp.float32)
         for h in (1, 0):
             for s in range(2):
@@ -320,6 +328,7 @@
             pltpu.VMEM((64, 128), f32),
             pltpu.VMEM((3, 2, 4, 4, 64, 128), bf16),
             pltpu.VMEM((3, 2, 4, 2, 64, 128), bf16),
+            pltpu.VMEM((3, 64, 128), bf16),
             pltpu.VMEM((3, 64, 128), bf16),
             pltpu.VMEM((2048, 128), bf16),
             pltpu.VMEM((144, 2048), bf16),

time: 73.7 us -> 78.6 us (1.066)
  Pallas kernels: 71.3 us -> 76.2 us
    pallas_call x1, Pallas kernels: 71.3 us -> 76.2 us  [body(): pl.pallas_call(pair_kernel, name='pairs', out_shape=jax.ShapeDtypeStruct(...]
where the time goes in v4:
time: 78.6 us; the launch traced here: 78.3 us
  Pallas kernels  76.2 us (97%)
  local copies, waits for them, and re-layouts  1.46 us (2%)
    pallas_call x1, Pallas kernels, body(): pl.pallas_call(pair_kernel, name='pairs', out_shape=jax.ShapeDtypeStruct(...  76.2 us

profile of v4, /device:TPU:1, one launch (start us, length us, event | category | flops | bytes accessed | tf_op | source)
XLA Modules:
  0.0 78.3 jit_solution(4575578287379108507)
XLA Ops:
  0.6 76.2 %pairs.1 = f32[256,128]{1,0:T(8,128)} custom-call(f32[64,128]{1,0:T(8,128)} %lp.1, f32[64,128]{1,0:T(8,128)} %rp.1, bf16[64,128]{1,0:T(8,128)(2,1)} %lc.1, bf16[64,128]{1,0:T(8,128)(2,1)} %rc.1), custom_call_target="tpu_custom_call" | custom-call | tf_op jit(solution)/shard_map/pairs/pallas_call | solution.py:320
  76.8 1.5 %fusion = (f32[64,128]{1,0:T(8,128)}, f32[64,128]{1,0:T(8,128)}, f32[64,128]{1,0:T(8,128)}, f32[64,128]{1,0:T(8,128)}) fusion(f32[256,128]{1,0:T(8,128)} %pairs.1), kind=kLoop, calls=%fused_computation | loop fusion | bytes 262144 | tf_op jit(solution)/shard_map/slice | solution.py:367

commit v5 on v3

--- a/solution.py
+++ b/solution.py
@@ -37,8 +37,10 @@
     z_down = [at(dz=-way * o) for o in Z_LEFT]
     z_far = {o: at(dz=o) for o in (-6, -2, 2, 6)}
 
+    z_on = (at(dz=4), at(dz=-4))
+
     barrier = pltpu.get_barrier_semaphore()
-    partners = [z_far[-6], z_far[6], z_far[-2], z_far[2], at(dz=1), at(dz=-1), *at_x[1:], *at_y[1:], sibling]
+    partners = [*z_on, z_far[-6], z_far[6], z_far[-2], z_far[2], at(dz=1), at(dz=-1), *at_x[1:], *at_y[1:], sibling]
     for p in partners:
         pl.semaphore_signal(barrier, inc=1, device_id=p, device_id_type=MESH)
 
@@ -84,6 +86,8 @@
 
     def r_z(ph, h, s):
         n = 2 * h + s
+        if h == 0:
+            return send(gr.at[ph, 1, 0, s], gr.at[ph, 0, 0, s], rz_s.at[ph, n], rz_r.at[ph, n], z_on[s])
         return send(own_r.at[ph], gr.at[ph, h, 0, s], rz_s.at[ph, n], rz_r.at[ph, n], z_far[-Z_RIGHT[h][s]])
 
     def r_y(ph, h, i):
@@ -91,12 +95,15 @@
         return send(gr.at[ph, h, 0], gr.at[ph, h, i], ry_s.at[ph, n], ry_r.at[ph, n], at_y[i])
 
     def gather_start(ph):
-        go(r_z(ph, 0, 0))
-        go(r_z(ph, 0, 1))
+        go(r_z(ph, 1, 0))
+        go(r_z(ph, 1, 1))
         for i in (3, 0, 2):
             go(l_z(ph, i))
-        go(r_z(ph, 1, 0))
-        go(r_z(ph, 1, 1))
+
+    def pass_on(ph):
+        for s in range(2):
+            r_z(ph, 1, s).wait_recv()
+            go(r_z(ph, 0, s))
 
     def relay_left(ph):
         for i in (0, 2, 3):
@@ -106,8 +113,9 @@
         go(l_k(ph, 0))
 
     def relay_right(ph, h):
-        r_z(ph, h, 0).wait_recv()
-        r_z(ph, h, 1).wait_recv()
+        if h == 0:
+            r_z(ph, 0, 0).wait_recv()
+            r_z(ph, 0, 1).wait_recv()
         for i in (2, 1, 3):
             go(r_y(ph, h, i))
 
@@ -216,7 +224,10 @@
         if st == 0:
             gather_start(2)
         else:
-            sent(7)
+            sent(5)
+        pass_on(st)
+        if st == 0:
+            pass_on(2)
         relay_left(st)
         relay_right(st, 1)
         prepare_left(st, 0, 0)

time: 73.7 us -> 76.2 us (1.034)
  Pallas kernels: 71.3 us -> 73.8 us
    pallas_call x1, Pallas kernels: 71.3 us -> 73.8 us  [body(): pl.pallas_call(pair_kernel, name='pairs', out_shape=jax.ShapeDtypeStruct(...]
where the time goes in v5:
time: 76.2 us; the launch traced here: 75.9 us
  Pallas kernels  73.8 us (97%)
  local copies, waits for them, and re-layouts  1.46 us (2%)
    pallas_call x1, Pallas kernels, body(): pl.pallas_call(pair_kernel, name='pairs', out_shape=jax.ShapeDtypeStruct(...  73.8 us

profile of v5, /device:TPU:1, one launch (start us, length us, event | category | flops | bytes accessed | tf_op | source)
XLA Modules:
  0.0 75.9 jit_solution(8032789169636613086)
XLA Ops:
  0.6 73.8 %pairs.1 = f32[256,128]{1,0:T(8,128)} custom-call(f32[64,128]{1,0:T(8,128)} %lp.1, f32[64,128]{1,0:T(8,128)} %rp.1, bf16[64,128]{1,0:T(8,128)(2,1)} %lc.1, bf16[64,128]{1,0:T(8,128)(2,1)} %rc.1), custom_call_target="tpu_custom_call" | custom-call | tf_op jit(solution)/shard_map/pairs/pallas_call | solution.py:323
  74.4 1.5 %fusion = (f32[64,128]{1,0:T(8,128)}, f32[64,128]{1,0:T(8,128)}, f32[64,128]{1,0:T(8,128)}, f32[64,128]{1,0:T(8,128)}) fusion(f32[256,128]{1,0:T(8,128)} %pairs.1), kind=kLoop, calls=%fused_computation | loop fusion | bytes 262144 | tf_op jit(solution)/shard_map/slice | solution.py:369
